TPU v7x, 32 devices: a whole 2x2x4 slice. The times are simulated.
32 devices in a mesh: ctx: 8 (over z, y), head: 4 (over x, core).
Axes of the slice: x: 2, y: 2, z: 4, core: 2. Of those that a mesh axis runs over, the one named last changes fastest.
Arguments:
- queries: bfloat16 [2048, 32, 128], P('ctx', 'head'), may hold values from -6 to 6
- key_states: bfloat16 [2048, 4, 128], P('ctx', 'head'), may hold values from -6 to 6
- value_states: bfloat16 [2048, 4, 128], P('ctx', 'head'), may hold values from -6 to 6
- doc_lengths: int32 [8], replicated, may hold values from 1 to 1792, 2048 in all
- grad_attended: bfloat16 [2048, 4096], P(('ctx', 'head')), may hold values from -6 to 6
Outputs:
- attended: bfloat16 [2048, 4096], P(('ctx', 'head'))
- grad_queries: bfloat16 [2048, 32, 128], P('ctx', 'head')
- grad_keys: bfloat16 [2048, 4, 128], P('ctx', 'head')
- grad_values: bfloat16 [2048, 4, 128], P('ctx', 'head')
All inputs are finite; a program needn't handle non-finite values.
Results may differ from a plain program's by a relative error of at most 0.022.
Values may be sent and summed in bfloat16 or wider, within the bound.
No kernel may reach another device: no remote copies, remote signals or barrier semaphores. Data moves between devices by JAX's collectives and lax.ppermute only.
A program may use at most 64 MiB of HBM per device.

v0:
```python
import functools
import math

import jax
import jax.numpy as jnp
from jax import lax
from jax.experimental import pallas as pl
from jax.experimental.pallas import tpu as pltpu
from jax.sharding import PartitionSpec as P

DOC_MOST = 1792
NEG_FILL = -1e30
TILE = 256
CHUNK = 128
LOG2_E = 1.4426950408889634
SMALL_VMEM = 8 * 1024 * 1024


def dot(a, b):
    return jnp.dot(a, b, preferred_element_type=jnp.float32)


def dot_nt(a, b):
    return lax.dot_general(a, b, (((1,), (1,)), ((), ())), preferred_element_type=jnp.float32)


def unit(size):
    rows = lax.broadcasted_iota(jnp.int32, (size, size), 0)
    return (rows == lax.broadcasted_iota(jnp.int32, (size, size), 1)).astype(jnp.bfloat16)


def twice(column):
    return jnp.concatenate([column, column], axis=1)


def attention_kernel(
    doc_ref,
    q_ref,
    own_ref,
    near_ref,
    *refs,
    back,
    whole,
    ranks,
    heads,
    width,
    scale,
):
    arrived, far, refs = refs[:back], refs[back : 2 * back], refs[2 * back :]
    grad_parts, refs = refs[:ranks], refs[ranks:]
    out_parts, refs = refs[:ranks], refs[ranks:]
    (
        dq_ref,
        *refs,
    ) = refs
    d_refs, refs = refs[:4], refs[4:]
    (
        do_ref,
        o_ref,
        q32,
        keys,
        values,
        q_rows,
        do_rows,
        q_cols,
        do_cols,
        scores,
        accum,
        dq_acc,
        top,
        delta,
        d_blocks,
    ) = refs
    tok = q_ref.shape[0]
    part_rows = tok // ranks
    docs = doc_ref.shape[0]
    ctx = lax.axis_index("ctx")
    rank = lax.axis_index("head")
    parity = lax.rem(ctx, 2)
    base = 0 if whole else (ctx - parity - 2 * back) * tok
    own = ctx if whole else 2 * back + parity

    def pair_of(k):
        return (ctx // 2) ^ k if whole else back - k

    small = unit(width)
    ones = jnp.ones((width, width), jnp.bfloat16)

    values[:, width:] = jnp.ones_like(values[:, width:])
    for k in range(back + 1):
        pair = pair_of(k)
        mine, other = (own_ref, near_ref) if k == 0 else (arrived[k - 1], far[k - 1])
        for ref, place in ((mine, 2 * pair + parity), (other, 2 * pair + 1 - parity)):
            at = pl.ds(pl.multiple_of(place * tok, tok), tok)
            keys[at, :] = ref[0:tok, :]
            values[at, 0:width] = ref[tok:, :]
    for k in range(ranks):
        at = pl.ds(pl.multiple_of((rank ^ k) * part_rows, part_rows), part_rows)
        do_ref[at, :] = grad_parts[k][...]

    q32[...] = q_ref[...].astype(jnp.float32)
    d_blocks[...] = jnp.zeros_like(d_blocks)

    def chunk_step(chunk, carry):
        here = pl.ds(pl.multiple_of(chunk * CHUNK, CHUNK), CHUNK)
        for j in range(heads):
            part = pl.ds(j * CHUNK, CHUNK)
            q_rows[part, :] = q32[here, j, :].astype(jnp.bfloat16)
            do_rows[part, :] = do_ref[here, j * width : (j + 1) * width]
        q_cols[...] = dot_nt(small, q_rows[...]).astype(jnp.bfloat16)
        do_cols[...] = dot_nt(small, do_rows[...]).astype(jnp.bfloat16)
        top[...] = jnp.full_like(top, NEG_FILL)

        t_first = base + own * TILE + chunk * CHUNK
        t_last = t_first + CHUNK - 1
        t_col = t_first + lax.broadcasted_iota(jnp.int32, (CHUNK, width), 0)
        end = jnp.int32(0)
        start_first, start_last = jnp.int32(0), jnp.int32(0)
        start_col = jnp.zeros((CHUNK, width), jnp.int32)
        for i in range(docs):
            end = end + doc_ref[i]
            start_first = jnp.where(end <= t_first, end, start_first)
            start_last = jnp.where(end <= t_last, end, start_last)
            start_col = jnp.where(t_col >= end, end, start_col)
        low = jnp.maximum(start_first - base, 0) // TILE
        clear = jnp.clip((start_last - base + TILE - 1) // TILE, low, own)

        def score_tile(i, masked):
            at = pl.ds(pl.multiple_of(i * TILE, TILE), TILE)
            tile = dot_nt(q_rows[...], keys[at, :]) * (scale * LOG2_E)
            if masked:
                s_row = base + i * TILE + lax.broadcasted_iota(jnp.int32, (CHUNK, TILE), 1)
                live = (s_row >= twice(start_col)) & (s_row <= twice(t_col))
                tile = jnp.concatenate(
                    [
                        jnp.where(live, tile[j * CHUNK : (j + 1) * CHUNK], NEG_FILL)
                        for j in range(heads)
                    ],
                    axis=0,
                )
            scores[i] = tile
            top[...] = jnp.maximum(top[...], jnp.maximum(tile[:, :width], tile[:, width:]))

        def edge_step(n, carry):
            score_tile(jnp.where(n < clear - low, low + n, own), True)
            return carry

        def inner_step(i, carry):
            score_tile(i, False)
            return carry

        lax.fori_loop(0, clear - low + 1, edge_step, 0)
        lax.fori_loop(clear, own, inner_step, 0)
        top[...] = jnp.broadcast_to(jnp.max(top[...], axis=1, keepdims=True), top.shape)
        accum[...] = jnp.zeros_like(accum)

        def weigh_step(i, carry):
            at = pl.ds(pl.multiple_of(i * TILE, TILE), TILE)
            weights = jnp.exp2(scores[i] - twice(top[...])).astype(jnp.bfloat16)
            accum[...] += dot(weights, values[at, :])
            return carry

        lax.fori_loop(low, own + 1, weigh_step, 0)
        total = accum[:, width:]
        out = (accum[:, 0:width] / total).astype(jnp.bfloat16)
        for j in range(heads):
            o_ref[here, j * width : (j + 1) * width] = out[j * CHUNK : (j + 1) * CHUNK]
        top[...] = top[...] + jnp.log2(total)
        product = do_rows[...].astype(jnp.float32) * out.astype(jnp.float32)
        coarse = product.astype(jnp.bfloat16)
        fine = (product - coarse.astype(jnp.float32)).astype(jnp.bfloat16)
        delta[...] = dot(coarse, ones) + dot(fine, ones)
        dq_acc[...] = jnp.zeros_like(dq_acc)

        def back_step(i, carry):
            at = pl.ds(pl.multiple_of(i * TILE, TILE), TILE)
            probs = jnp.exp2(scores[i] - twice(top[...]))
            d_probs = dot_nt(do_rows[...], values[at, 0:width])
            d_scores = (probs * (d_probs - twice(delta[...]))).astype(jnp.bfloat16)
            dq_acc[...] += dot(d_scores, keys[at, :])
            d_blocks[i, 0:width, :] += dot(q_cols[...], d_scores)
            d_blocks[i, width:, :] += dot(do_cols[...], probs.astype(jnp.bfloat16))
            return carry

        lax.fori_loop(low, own + 1, back_step, 0)
        for j in range(heads):
            q32[here, j, :] = dq_acc[j * CHUNK : (j + 1) * CHUNK, :] * scale
        return carry

    lax.fori_loop(0, tok // CHUNK, chunk_step, 0)
    for k in range(ranks):
        at = pl.ds(pl.multiple_of((rank ^ k) * part_rows, part_rows), part_rows)
        out_parts[k][...] = o_ref[at, :]
    dq_ref[...] = q32[...].astype(jnp.bfloat16)
    for k in range(back + 1):
        mine, other = 2 * pair_of(k) + parity, 2 * pair_of(k) + 1 - parity
        which, to = (0, back - k) if k > 1 else (2, k)
        d_refs[which][to, 0:width, :] = d_blocks[mine, 0:width, :] * scale
        d_refs[which][to, width:, :] = d_blocks[mine, width:, :]
        d_refs[which + 1][to, 0:width, :] = (d_blocks[other, 0:width, :] * scale).astype(
            jnp.bfloat16
        )
        d_refs[which + 1][to, width:, :] = d_blocks[other, width:, :].astype(jnp.bfloat16)


def attend(doc_lengths, queries, own, near, arrived, far, grad_parts, whole):
    tok, heads, width = queries.shape
    back = len(arrived)
    ranks = len(grad_parts)
    tiles = 2 * (back + 1)
    span = tiles * tok
    rows = heads * CHUNK
    vmem = pl.BlockSpec(memory_space=pltpu.VMEM)
    smem = pl.BlockSpec(memory_space=pltpu.SMEM)
    out_part = jax.ShapeDtypeStruct((tok // ranks, heads * width), jnp.bfloat16)
    return pl.pallas_call(
        functools.partial(
            attention_kernel,
            back=back,
            whole=whole,
            ranks=ranks,
            heads=heads,
            width=width,
            scale=1.0 / math.sqrt(width),
        ),
        out_shape=[out_part] * ranks
        + [
            jax.ShapeDtypeStruct((tok, heads, width), jnp.bfloat16),
        ]
        + [
            jax.ShapeDtypeStruct((size, 2 * width, tok), dtype)
            for size in (back - 1, 2)
            for dtype in (jnp.float32, jnp.bfloat16)
        ],
        in_specs=[smem] + [vmem] * (3 + 2 * back + ranks),
        out_specs=[vmem] * (ranks + 5),
        scratch_shapes=[
            pltpu.VMEM((tok, heads * width), jnp.bfloat16),
            pltpu.VMEM((tok, heads * width), jnp.bfloat16),
            pltpu.VMEM((tok, heads, width), jnp.float32),
            pltpu.VMEM((span, width), jnp.bfloat16),
            pltpu.VMEM((span, 2 * width), jnp.bfloat16),
            pltpu.VMEM((rows, width), jnp.bfloat16),
            pltpu.VMEM((rows, width), jnp.bfloat16),
            pltpu.VMEM((width, rows), jnp.bfloat16),
            pltpu.VMEM((width, rows), jnp.bfloat16),
            pltpu.VMEM((tiles, rows, TILE), jnp.float32),
            pltpu.VMEM((rows, 2 * width), jnp.float32),
            pltpu.VMEM((rows, width), jnp.float32),
            pltpu.VMEM((rows, width), jnp.float32),
            pltpu.VMEM((rows, width), jnp.float32),
            pltpu.VMEM((tiles, 2 * width, tok), jnp.float32),
        ],
        compiler_params=pltpu.CompilerParams(vmem_limit_bytes=40 * 1024 * 1024),
        cost_estimate=pl.CostEstimate(
            flops=14 * tok * heads * width * span,
            bytes_accessed=4 * tok * heads * width * 2 + 4 * span * width * 2,
            transcendentals=tok * heads * span,
        ),
        name="attention",
    )(doc_lengths, queries, own, near, *arrived, *far, *grad_parts)


def split_kernel(grad_ref, *part_refs):
    size = part_refs[0].shape[1]
    for k, ref in enumerate(part_refs):
        at = pl.multiple_of((lax.axis_index("head") ^ k) * size, size)
        ref[...] = grad_ref[:, pl.ds(at, size)]


def split(grad_attended, ranks):
    rows, columns = grad_attended.shape
    vmem = pl.BlockSpec(memory_space=pltpu.VMEM)
    part = jax.ShapeDtypeStruct((rows, columns // ranks), grad_attended.dtype)
    return pl.pallas_call(
        split_kernel,
        out_shape=[part] * ranks,
        in_specs=[vmem],
        out_specs=[vmem] * ranks,
        compiler_params=pltpu.CompilerParams(vmem_limit_bytes=SMALL_VMEM),
        name="split",
    )(grad_attended)


def join_kernel(*refs):
    out_ref = refs[-1]
    size = refs[0].shape[1]
    for k, ref in enumerate(refs[:-1]):
        at = pl.multiple_of((lax.axis_index("head") ^ k) * size, size)
        out_ref[:, pl.ds(at, size)] = ref[...]


def join(parts):
    rows, size = parts[0].shape
    vmem = pl.BlockSpec(memory_space=pltpu.VMEM)
    return pl.pallas_call(
        join_kernel,
        out_shape=jax.ShapeDtypeStruct((rows, size * len(parts)), parts[0].dtype),
        in_specs=[vmem] * len(parts),
        out_specs=vmem,
        compiler_params=pltpu.CompilerParams(vmem_limit_bytes=SMALL_VMEM),
        name="join",
    )(*parts)


def merge_kernel(mine_ref, other_ref, *block_refs):
    for k, ref in enumerate(block_refs):
        ref[...] = (mine_ref[k] + other_ref[k].astype(jnp.float32)).astype(ref.dtype)


def merge(mine, other, dtypes):
    vmem = pl.BlockSpec(memory_space=pltpu.VMEM)
    return pl.pallas_call(
        merge_kernel,
        out_shape=[jax.ShapeDtypeStruct(mine.shape[1:], dtype) for dtype in dtypes],
        in_specs=[vmem, vmem],
        out_specs=[vmem] * len(dtypes),
        compiler_params=pltpu.CompilerParams(vmem_limit_bytes=SMALL_VMEM),
        name="merge",
    )(mine, other)


def finish_kernel(own_ref, *refs):
    arrived = refs[:-2]
    dk_ref, dv_ref = refs[-2:]
    total = own_ref[...]
    for ref in arrived:
        total = total + ref[...].astype(jnp.float32)
    total = total.astype(jnp.bfloat16)
    width = dk_ref.shape[1]
    large = unit(dk_ref.shape[0])
    dk_ref[...] = dot_nt(large, total[:width]).astype(jnp.bfloat16)
    dv_ref[...] = dot_nt(large, total[width:]).astype(jnp.bfloat16)


def finish(own_part, arrived):
    both, tok = own_part.shape
    vmem = pl.BlockSpec(memory_space=pltpu.VMEM)
    shape = jax.ShapeDtypeStruct((tok, both // 2), jnp.bfloat16)
    return pl.pallas_call(
        finish_kernel,
        out_shape=(shape, shape),
        in_specs=[vmem] * (1 + len(arrived)),
        out_specs=(vmem, vmem),
        compiler_params=pltpu.CompilerParams(vmem_limit_bytes=SMALL_VMEM),
        name="finish",
    )(own_part, *arrived)


def shifted(block, by, count):
    pairs = [(i, i + by) for i in range(count) if 0 <= i + by < count]
    return lax.ppermute(block, "ctx", pairs)


def exchanged(block, axis, by):
    return lax.ppermute(block, axis, [(i, i ^ by) for i in range(lax.axis_size(axis))])


def after(value, *others):
    return lax.optimization_barrier((value, *others))


def body(queries, key_states, value_states, doc_lengths, grad_attended):
    tok, heads, width = queries.shape
    count = lax.axis_size("ctx")
    ranks = lax.axis_size("head")
    reach = min((DOC_MOST + tok - 2) // tok, count - 1)
    back = min((reach + 1) // 2, count // 2 - 1)
    whole = count == 8 and back == 3
    own = jnp.concatenate(
        [key_states.reshape(tok, width), value_states.reshape(tok, width)], axis=0
    )
    if whole:
        across, beside = exchanged(own, "ctx", 4), exchanged(own, "ctx", 2)
    else:
        arrived = [shifted(own, 2 * k, count) for k in range(1, back + 1)]
    near = exchanged(own, "ctx", 1)
    grads = split(grad_attended, ranks)
    grads = [part if k == 0 else exchanged(part, "head", k) for k, part in enumerate(grads)]
    if whole:
        beside, near = after(beside, near)
        far_beside = exchanged(beside, "ctx", 1)
        across, far_beside, *grads[1:3] = after(across, far_beside, *grads[1:3])
        passed = exchanged(across, "ctx", 2)
        far_across = exchanged(across, "ctx", 1)
        passed, *grads[3:] = after(passed, *grads[3:])
        far_passed = exchanged(passed, "ctx", 1)
        arrived = [beside, across, passed]
        far = [far_beside, far_across, far_passed]
    else:
        far = [exchanged(block, "ctx", 1) for block in arrived]
    outputs = attend(
        doc_lengths, queries, own, near, arrived, far, grads, whole
    )

    def home(block, k):
        return exchanged(block, "ctx", 2 * k) if whole else shifted(block, -2 * k, count)

    outs, grad_queries = list(outputs[:ranks]), outputs[ranks]
    mine_far, other_far, mine_rest, other_rest = outputs[ranks + 1 :]
    other_far = exchanged(other_far, "ctx", 1)
    other_rest = exchanged(other_rest, "ctx", 1)
    outs[1:] = [exchanged(part, "head", k + 1) for k, part in enumerate(outs[1:])]
    other_far, *outs[1:3] = after(other_far, *outs[1:3])
    blocks = merge(mine_far, other_far, [jnp.bfloat16] * (back - 1))
    returned = [home(block, back - n) for n, block in enumerate(blocks)]
    other_rest, returned[0] = after(other_rest, returned[0])
    own_block, block = merge(mine_rest, other_rest, [jnp.float32, jnp.bfloat16])
    returned.append(home(block, 1))
    grad_keys, grad_values = finish(own_block, returned)
    attended = join(outs)
    grad_keys = grad_keys.reshape(tok, 1, width)
    grad_values = grad_values.reshape(tok, 1, width)
    return attended, grad_queries, grad_keys, grad_values


def solution(mesh):
    in_specs = (
        P("ctx", "head", None),
        P("ctx", "head", None),
        P("ctx", "head", None),
        P(),
        P(("ctx", "head"), None),
    )
    out_specs = (
        P(("ctx", "head"), None),
        P("ctx", "head", None),
        P("ctx", "head", None),
        P("ctx", "head", None),
    )
    return jax.shard_map(body, mesh=mesh, in_specs=in_specs, out_specs=out_specs, check_vma=False)
```

profile of v0, /device:TPU:0, one launch (start us, length us, event | category | flops | bytes accessed | tf_op | source)
XLA Modules:
  0.0 73.4 jit_solution(1158363648062950650)
XLA Ops:
  0.6 0.9 %pad_maximum_fusion.own_ref = bf16[512,128]{1,0:T(8,128)(2,1)S(1)} fusion(bf16[256,128]{1,0:T(8,128)(2,1)} %bitcast.4, bf16[256,128]{1,0:T(8,128)(2,1)} %bitcast.5), kind=kLoop, calls=%fused_computation | loop fusion | flops 262144 | bytes 262144 | tf_op jit(solution)/shard_map/concatenate | solution.py:370
  1.5 3.0 %collective-permute-start.1 = (bf16[512,128]{1,0:T(8,128)(2,1)S(1)}, bf16[512,128]{1,0:T(8,128)(2,1)S(1)}, u32[]{:S(2)}, u32[]{:S(2)}) collective-permute-start(bf16[512,128]{1,0:T(8,128)(2,1)S(1)} %pad_maximum_fusion.own_ref), channel_id=1, source_target_pairs={{0,4},{4,0},{8,12},{12,8},{16,20},{20,16},{24,28},{28,24},{1,5},{5... | collective-permute-start | bytes 393224 | tf_op jit(solution)/shard_map/ppermute | solution.py:356
  4.5 1.6 %collective-permute-start = (bf16[512,128]{1,0:T(8,128)(2,1)S(1)}, bf16[512,128]{1,0:T(8,128)(2,1)S(1)}, u32[]{:S(2)}, u32[]{:S(2)}) collective-permute-start(bf16[512,128]{1,0:T(8,128)(2,1)S(1)} %pad_maximum_fusion.own_ref), channel_id=1, source_target_pairs={{0,8},{4,12},{8,0},{12,4},{16,24},{20,28},{24,16},{28,20},{1,9},{5... | collective-permute-start | bytes 393224 | tf_op jit(solution)/shard_map/ppermute | solution.py:356
  6.1 2.6 %collective-permute-start.2 = (bf16[512,128]{1,0:T(8,128)(2,1)S(1)}, bf16[512,128]{1,0:T(8,128)(2,1)S(1)}, u32[]{:S(2)}, u32[]{:S(2)}) collective-permute-start(bf16[512,128]{1,0:T(8,128)(2,1)S(1)} %pad_maximum_fusion.own_ref), channel_id=1, source_target_pairs={{0,16},{4,20},{8,24},{12,28},{16,0},{20,4},{24,8},{28,12},{1,17},{... | collective-permute-start | bytes 393224 | tf_op jit(solution)/shard_map/ppermute | solution.py:356
  8.7 0.0 copy-start
  8.7 1.0 %copy-done = bf16[64,4096]{1,0:T(8,128)(2,1)S(1)} copy-done((bf16[64,4096]{1,0:T(8,128)(2,1)S(1)}, bf16[64,4096]{1,0:T(8,128)(2,1)}, u32[]{:S(2)}) %copy-start) | copy-done | bytes 524312
  9.8 0.0 copy-start.1
  9.8 0.1 collective-permute-start.4
  9.9 1.6 %collective-permute-start.5 = (bf16[64,1024]{1,0:T(8,128)(2,1)S(1)}, bf16[64,1024]{1,0:T(8,128)(2,1)S(1)}, u32[]{:S(2)}, u32[]{:S(2)}) collective-permute-start(bf16[64,1024]{1,0:T(8,128)(2,1)S(1)} %get-tuple-element.39), channel_id=1, source_target_pairs={{0,2},{1,3},{2,0},{3,1},{4,6},{5,7},{6,4},{7,5},{8,10},{9,11},{10,... | collective-permute-start | bytes 393224 | tf_op jit(solution)/shard_map/ppermute | solution.py:356
  11.4 0.0 collective-permute-done.1.near_ref
  11.4 0.0 collective-permute-done.refs_0_
  11.4 0.5 collective-permute-start.3
  11.9 0.0 copy-start.2
  11.9 0.0 collective-permute-start.7
  12.0 2.6 %collective-permute-done.2.refs_1_ = bf16[512,128]{1,0:T(8,128)(2,1)S(1)} collective-permute-done((bf16[512,128]{1,0:T(8,128)(2,1)S(1)}, bf16[512,128]{1,0:T(8,128)(2,1)S(1)}, u32[]{:S(2)}, u32[]{:S(2)}) %collective-permute-start.2) | collective-permute-done | bytes 131104 | tf_op jit(solution)/shard_map/ppermute | solution.py:356
  14.6 0.0 collective-permute-done.4.refs_7_
  14.6 1.7 %collective-permute-done.5.refs_8_ = bf16[64,1024]{1,0:T(8,128)(2,1)S(1)} collective-permute-done((bf16[64,1024]{1,0:T(8,128)(2,1)S(1)}, bf16[64,1024]{1,0:T(8,128)(2,1)S(1)}, u32[]{:S(2)}, u32[]{:S(2)}) %collective-permute-start.5) | collective-permute-done | bytes 131104 | tf_op jit(solution)/shard_map/ppermute | solution.py:356
  16.2 0.8 %collective-permute-done.3.refs_3_ = bf16[512,128]{1,0:T(8,128)(2,1)S(1)} collective-permute-done((bf16[512,128]{1,0:T(8,128)(2,1)S(1)}, bf16[512,128]{1,0:T(8,128)(2,1)S(1)}, u32[]{:S(2)}, u32[]{:S(2)}) %collective-permute-start.3) | collective-permute-done | bytes 131104 | tf_op jit(solution)/shard_map/ppermute | solution.py:356
  17.0 0.4 collective-permute-start.6
  17.5 0.5 collective-permute-start.8
  18.0 0.2 collective-permute-done.7.refs_9_
  18.1 3.8 %collective-permute-done.6.refs_2_ = bf16[512,128]{1,0:T(8,128)(2,1)S(1)} collective-permute-done((bf16[512,128]{1,0:T(8,128)(2,1)S(1)}, bf16[512,128]{1,0:T(8,128)(2,1)S(1)}, u32[]{:S(2)}, u32[]{:S(2)}) %collective-permute-start.6) | collective-permute-done | bytes 131104 | tf_op jit(solution)/shard_map/ppermute | solution.py:356
  22.0 0.5 collective-permute-start.9
  22.5 0.0 collective-permute-done.8.refs_4_
  22.5 4.5 %collective-permute-done.9.refs_5_ = bf16[512,128]{1,0:T(8,128)(2,1)S(1)} collective-permute-done((bf16[512,128]{1,0:T(8,128)(2,1)S(1)}, bf16[512,128]{1,0:T(8,128)(2,1)S(1)}, u32[]{:S(2)}, u32[]{:S(2)}) %collective-permute-start.9) | collective-permute-done | bytes 131104 | tf_op jit(solution)/shard_map/ppermute | solution.py:356
  26.9 0.0 copy-done.1
  26.9 0.0 copy-done.2
  27.0 8.3 %attention.1 = (bf16[64,1024]{1,0:T(8,128)(2,1)S(1)}, bf16[64,1024]{1,0:T(8,128)(2,1)S(1)}, bf16[64,1024]{1,0:T(8,128)(2,1)S(1)}, bf16[64,1024]{1,0:T(8,128)(2,1...) custom-call(s32[8]{0:T(128)S(1)} %copy-done.2, ...), custom_call_target="tpu_custom_call" | custom-call | flops 7516192768 | bytes 4194304 | tf_op jit(solution)/shard_map/attention/pallas_call | solution.py:216
  35.2 3.1 %collective-permute-start.10 = (bf16[2,256,256]{2,1,0:T(8,128)(2,1)S(1)}, bf16[2,256,256]{2,1,0:T(8,128)(2,1)S(1)}, u32[]{:S(2)}, u32[]{:S(2)}) collective-permute-start(bf16[2,256,256]{2,1,0:T(8,128)(2,1)S(1)} %get-tuple-element.49), channel_id=1, source_target_pairs={{0,4},{4,0},{8,12},{12,8},{16,20},{20,16},{24,28},{28,24},{1,5},{5... | collective-permute-start | bytes 786440 | tf_op jit(solution)/shard_map/ppermute | solution.py:356
  38.3 0.0 collective-permute-start.11
  38.3 0.7 collective-permute-start.12
  39.0 0.0 collective-permute-start.14
  39.0 0.6 collective-permute-done.11.refs_1_
  39.7 4.6 %collective-permute-done.12.refs_2_ = bf16[64,1024]{1,0:T(8,128)(2,1)S(1)} collective-permute-done((bf16[64,1024]{1,0:T(8,128)(2,1)S(1)}, bf16[64,1024]{1,0:T(8,128)(2,1)S(1)}, u32[]{:S(2)}, u32[]{:S(2)}) %collective-permute-start.12) | collective-permute-done | bytes 131104 | tf_op jit(solution)/shard_map/ppermute | solution.py:356
  44.2 0.5 collective-permute-done.10.other_ref
  44.8 0.1 merge.2
  44.9 16.8 %collective-permute-start.15 = (bf16[256,256]{1,0:T(8,128)(2,1)S(1)}, bf16[256,256]{1,0:T(8,128)(2,1)S(1)}, u32[]{:S(2)}, u32[]{:S(2)}) collective-permute-start(bf16[256,256]{1,0:T(8,128)(2,1)S(1)} %get-tuple-element.60), channel_id=1, source_target_pairs={{0,24},{4,28},{8,16},{12,20},{16,8},{20,12},{24,0},{28,4},{1,25},{... | collective-permute-start | bytes 393224 | tf_op jit(solution)/shard_map/ppermute | solution.py:356
  61.6 0.0 collective-permute-start.13
  61.6 0.0 collective-permute-start.16
  61.6 0.0 collective-permute-done.14.other_ref
  61.6 2.9 %collective-permute-done.15.refs_0_ = bf16[256,256]{1,0:T(8,128)(2,1)S(1)} collective-permute-done((bf16[256,256]{1,0:T(8,128)(2,1)S(1)}, bf16[256,256]{1,0:T(8,128)(2,1)S(1)}, u32[]{:S(2)}, u32[]{:S(2)}) %collective-permute-start.15) | collective-permute-done | bytes 131104 | tf_op jit(solution)/shard_map/ppermute | solution.py:356
  64.6 0.1 collective-permute-start.17
  64.7 1.7 %collective-permute-done.13.refs_3_ = bf16[64,1024]{1,0:T(8,128)(2,1)S(1)} collective-permute-done((bf16[64,1024]{1,0:T(8,128)(2,1)S(1)}, bf16[64,1024]{1,0:T(8,128)(2,1)S(1)}, u32[]{:S(2)}, u32[]{:S(2)}) %collective-permute-start.13) | collective-permute-done | bytes 131104 | tf_op jit(solution)/shard_map/ppermute | solution.py:356
  66.4 0.8 %join.1 = bf16[64,4096]{1,0:T(8,128)(2,1)} custom-call(bf16[64,1024]{1,0:T(8,128)(2,1)S(1)} %get-tuple-element.48.refs_0_, bf16[64,1024]{1,0:T(8,128)(2,1)S(1)} %collective-permute-done.11.refs_1_, bf16[64,1024]{1,0:T(8,128)(2,1)S(1)} %collective-permute-done.12.refs_2_, bf16[64,1024]{1,0:T(8,128)(2,1)S(1)} %collective-permute-done.13.refs_3_), custom_call_target="tpu_custom_call" | custom-call | tf_op jit(solution)/shard_map/join/pallas_call | solution.py:296
  67.2 2.7 %collective-permute-done.16.refs_1_ = bf16[256,256]{1,0:T(8,128)(2,1)S(1)} collective-permute-done((bf16[256,256]{1,0:T(8,128)(2,1)S(1)}, bf16[256,256]{1,0:T(8,128)(2,1)S(1)}, u32[]{:S(2)}, u32[]{:S(2)}) %collective-permute-start.16) | collective-permute-done | bytes 131104 | tf_op jit(solution)/shard_map/ppermute | solution.py:356
  70.0 2.5 %collective-permute-done.17.refs_2_ = bf16[256,256]{1,0:T(8,128)(2,1)S(1)} collective-permute-done((bf16[256,256]{1,0:T(8,128)(2,1)S(1)}, bf16[256,256]{1,0:T(8,128)(2,1)S(1)}, u32[]{:S(2)}, u32[]{:S(2)}) %collective-permute-start.17) | collective-permute-done | bytes 131104 | tf_op jit(solution)/shard_map/ppermute | solution.py:356
  72.5 0.9 %finish.1 = (bf16[256,128]{1,0:T(8,128)(2,1)}, bf16[256,128]{1,0:T(8,128)(2,1)}) custom-call(f32[256,256]{1,0:T(8,128)S(1)} %get-tuple-element.62.own_ref, bf16[256,256]{1,0:T(8,128)(2,1)S(1)} %collective-permute-done.15.refs_0_, bf16[256,256]{1,0:T(8,128)(2,1)S(1)} %collective-permute-done.16.refs_1_, bf16[256,256]{1,0:T(8,128)(2,1)S(1)} %collective-permute-done.17.refs_2_), custom_call_target="tpu_custom_call" | custom-call | tf_op jit(solution)/shard_map/finish/pallas_call | solution.py:340
  (2 shorter events, 0.1 us)
Async XLA Ops:
  1.5 9.9 %collective-permute-start.1 = (bf16[512,128]{1,0:T(8,128)(2,1)S(1)}, bf16[512,128]{1,0:T(8,128)(2,1)S(1)}, u32[]{:S(2)}, u32[]{:S(2)}) collective-permute-start(bf16[512,128]{1,0:T(8,128)(2,1)S(1)} %pad_maximum_fusion.own_ref), channel_id=1, source_target_pairs={{0,4},{4,0},{8,12},{12,8},{16,20},{20,16},{24,28},{28,24},{1,5},{5... | collective-permute-start | bytes 393224 | tf_op jit(solution)/shard_map/ppermute | solution.py:356
  4.5 6.9 %collective-permute-start = (bf16[512,128]{1,0:T(8,128)(2,1)S(1)}, bf16[512,128]{1,0:T(8,128)(2,1)S(1)}, u32[]{:S(2)}, u32[]{:S(2)}) collective-permute-start(bf16[512,128]{1,0:T(8,128)(2,1)S(1)} %pad_maximum_fusion.own_ref), channel_id=1, source_target_pairs={{0,8},{4,12},{8,0},{12,4},{16,24},{20,28},{24,16},{28,20},{1,9},{5... | collective-permute-start | bytes 393224 | tf_op jit(solution)/shard_map/ppermute | solution.py:356
  6.1 8.4 %collective-permute-start.2 = (bf16[512,128]{1,0:T(8,128)(2,1)S(1)}, bf16[512,128]{1,0:T(8,128)(2,1)S(1)}, u32[]{:S(2)}, u32[]{:S(2)}) collective-permute-start(bf16[512,128]{1,0:T(8,128)(2,1)S(1)} %pad_maximum_fusion.own_ref), channel_id=1, source_target_pairs={{0,16},{4,20},{8,24},{12,28},{16,0},{20,4},{24,8},{28,12},{1,17},{... | collective-permute-start | bytes 393224 | tf_op jit(solution)/shard_map/ppermute | solution.py:356
  8.7 1.0 %copy-start = (bf16[64,4096]{1,0:T(8,128)(2,1)S(1)}, bf16[64,4096]{1,0:T(8,128)(2,1)}, u32[]{:S(2)}) copy-start(bf16[64,4096]{1,0:T(8,128)(2,1)} %grad_ref.1) | copy-start | bytes 1572868
  9.8 17.2 %copy-start.1 = (bf16[256,8,128]{2,1,0:T(8,128)(2,1)S(1)}, bf16[256,8,128]{2,1,0:T(8,128)(2,1)}, u32[]{:S(2)}) copy-start(bf16[256,8,128]{2,1,0:T(8,128)(2,1)} %q_ref.1) | copy-start | bytes 1572868
  9.8 4.8 %collective-permute-start.4 = (bf16[64,1024]{1,0:T(8,128)(2,1)S(1)}, bf16[64,1024]{1,0:T(8,128)(2,1)S(1)}, u32[]{:S(2)}, u32[]{:S(2)}) collective-permute-start(bf16[64,1024]{1,0:T(8,128)(2,1)S(1)} %get-tuple-element.38), channel_id=1, source_target_pairs={{0,1},{1,0},{2,3},{3,2},{4,5},{5,4},{6,7},{7,6},{8,9},{9,8},{10,11... | collective-permute-start | bytes 393224 | tf_op jit(solution)/shard_map/ppermute | solution.py:356
  9.9 6.4 %collective-permute-start.5 = (bf16[64,1024]{1,0:T(8,128)(2,1)S(1)}, bf16[64,1024]{1,0:T(8,128)(2,1)S(1)}, u32[]{:S(2)}, u32[]{:S(2)}) collective-permute-start(bf16[64,1024]{1,0:T(8,128)(2,1)S(1)} %get-tuple-element.39), channel_id=1, source_target_pairs={{0,2},{1,3},{2,0},{3,1},{4,6},{5,7},{6,4},{7,5},{8,10},{9,11},{10,... | collective-permute-start | bytes 393224 | tf_op jit(solution)/shard_map/ppermute | solution.py:356
  11.4 5.6 %collective-permute-start.3 = (bf16[512,128]{1,0:T(8,128)(2,1)S(1)}, bf16[512,128]{1,0:T(8,128)(2,1)S(1)}, u32[]{:S(2)}, u32[]{:S(2)}) collective-permute-start(bf16[512,128]{1,0:T(8,128)(2,1)S(1)} %collective-permute-done.refs_0_), channel_id=1, source_target_pairs={{0,4},{4,0},{8,12},{12,8},{16,20},{20,16},{24,28},{28,24},{1,5},{5... | collective-permute-start | bytes 393224 | tf_op jit(solution)/shard_map/ppermute | solution.py:356
  11.9 15.0 %copy-start.2 = (s32[8]{0:T(128)S(1)}, s32[8]{0:T(128)}, u32[]{:S(2)}) copy-start(s32[8]{0:T(128)} %doc_ref.1) | copy-start | bytes 100
  11.9 6.2 %collective-permute-start.7 = (bf16[64,1024]{1,0:T(8,128)(2,1)S(1)}, bf16[64,1024]{1,0:T(8,128)(2,1)S(1)}, u32[]{:S(2)}, u32[]{:S(2)}) collective-permute-start(bf16[64,1024]{1,0:T(8,128)(2,1)S(1)} %get-tuple-element.41), channel_id=1, source_target_pairs={{0,3},{1,2},{2,1},{3,0},{4,7},{5,6},{6,5},{7,4},{8,11},{9,10},{10,... | collective-permute-start | bytes 393224 | tf_op jit(solution)/shard_map/ppermute | solution.py:356
  17.0 5.0 %collective-permute-start.6 = (bf16[512,128]{1,0:T(8,128)(2,1)S(1)}, bf16[512,128]{1,0:T(8,128)(2,1)S(1)}, u32[]{:S(2)}, u32[]{:S(2)}) collective-permute-start(bf16[512,128]{1,0:T(8,128)(2,1)S(1)} %collective-permute-done.2.refs_1_), channel_id=1, source_target_pairs={{0,8},{4,12},{8,0},{12,4},{16,24},{20,28},{24,16},{28,20},{1,9},{5... | collective-permute-start | bytes 393224 | tf_op jit(solution)/shard_map/ppermute | solution.py:356
  17.5 5.0 %collective-permute-start.8 = (bf16[512,128]{1,0:T(8,128)(2,1)S(1)}, bf16[512,128]{1,0:T(8,128)(2,1)S(1)}, u32[]{:S(2)}, u32[]{:S(2)}) collective-permute-start(bf16[512,128]{1,0:T(8,128)(2,1)S(1)} %collective-permute-done.2.refs_1_), channel_id=1, source_target_pairs={{0,4},{4,0},{8,12},{12,8},{16,20},{20,16},{24,28},{28,24},{1,5},{5... | collective-permute-start | bytes 393224 | tf_op jit(solution)/shard_map/ppermute | solution.py:356
  22.0 5.0 %collective-permute-start.9 = (bf16[512,128]{1,0:T(8,128)(2,1)S(1)}, bf16[512,128]{1,0:T(8,128)(2,1)S(1)}, u32[]{:S(2)}, u32[]{:S(2)}) collective-permute-start(bf16[512,128]{1,0:T(8,128)(2,1)S(1)} %collective-permute-done.6.refs_2_), channel_id=1, source_target_pairs={{0,4},{4,0},{8,12},{12,8},{16,20},{20,16},{24,28},{28,24},{1,5},{5... | collective-permute-start | bytes 393224 | tf_op jit(solution)/shard_map/ppermute | solution.py:356
  35.2 9.5 %collective-permute-start.10 = (bf16[2,256,256]{2,1,0:T(8,128)(2,1)S(1)}, bf16[2,256,256]{2,1,0:T(8,128)(2,1)S(1)}, u32[]{:S(2)}, u32[]{:S(2)}) collective-permute-start(bf16[2,256,256]{2,1,0:T(8,128)(2,1)S(1)} %get-tuple-element.49), channel_id=1, source_target_pairs={{0,4},{4,0},{8,12},{12,8},{16,20},{20,16},{24,28},{28,24},{1,5},{5... | collective-permute-start | bytes 786440 | tf_op jit(solution)/shard_map/ppermute | solution.py:356
  38.3 1.3 %collective-permute-start.11 = (bf16[64,1024]{1,0:T(8,128)(2,1)S(1)}, bf16[64,1024]{1,0:T(8,128)(2,1)S(1)}, u32[]{:S(2)}, u32[]{:S(2)}) collective-permute-start(bf16[64,1024]{1,0:T(8,128)(2,1)S(1)} %get-tuple-element.50), channel_id=1, source_target_pairs={{0,1},{1,0},{2,3},{3,2},{4,5},{5,4},{6,7},{7,6},{8,9},{9,8},{10,11... | collective-permute-start | bytes 393224 | tf_op jit(solution)/shard_map/ppermute | solution.py:356
  38.3 5.9 %collective-permute-start.12 = (bf16[64,1024]{1,0:T(8,128)(2,1)S(1)}, bf16[64,1024]{1,0:T(8,128)(2,1)S(1)}, u32[]{:S(2)}, u32[]{:S(2)}) collective-permute-start(bf16[64,1024]{1,0:T(8,128)(2,1)S(1)} %get-tuple-element.51), channel_id=1, source_target_pairs={{0,2},{1,3},{2,0},{3,1},{4,6},{5,7},{6,4},{7,5},{8,10},{9,11},{10,... | collective-permute-start | bytes 393224 | tf_op jit(solution)/shard_map/ppermute | solution.py:356
  39.0 22.6 %collective-permute-start.14 = (bf16[2,256,256]{2,1,0:T(8,128)(2,1)S(1)}, bf16[2,256,256]{2,1,0:T(8,128)(2,1)S(1)}, u32[]{:S(2)}, u32[]{:S(2)}) collective-permute-start(bf16[2,256,256]{2,1,0:T(8,128)(2,1)S(1)} %get-tuple-element.57), channel_id=1, source_target_pairs={{0,4},{4,0},{8,12},{12,8},{16,20},{20,16},{24,28},{28,24},{1,5},{5... | collective-permute-start | bytes 786440 | tf_op jit(solution)/shard_map/ppermute | solution.py:356
  44.9 19.7 %collective-permute-start.15 = (bf16[256,256]{1,0:T(8,128)(2,1)S(1)}, bf16[256,256]{1,0:T(8,128)(2,1)S(1)}, u32[]{:S(2)}, u32[]{:S(2)}) collective-permute-start(bf16[256,256]{1,0:T(8,128)(2,1)S(1)} %get-tuple-element.60), channel_id=1, source_target_pairs={{0,24},{4,28},{8,16},{12,20},{16,8},{20,12},{24,0},{28,4},{1,25},{... | collective-permute-start | bytes 393224 | tf_op jit(solution)/shard_map/ppermute | solution.py:356
  61.6 4.8 %collective-permute-start.13 = (bf16[64,1024]{1,0:T(8,128)(2,1)S(1)}, bf16[64,1024]{1,0:T(8,128)(2,1)S(1)}, u32[]{:S(2)}, u32[]{:S(2)}) collective-permute-start(bf16[64,1024]{1,0:T(8,128)(2,1)S(1)} %get-tuple-element.54), channel_id=1, source_target_pairs={{0,3},{1,2},{2,1},{3,0},{4,7},{5,6},{6,5},{7,4},{8,11},{9,10},{10,... | collective-permute-start | bytes 393224 | tf_op jit(solution)/shard_map/ppermute | solution.py:356
  61.6 8.3 %collective-permute-start.16 = (bf16[256,256]{1,0:T(8,128)(2,1)S(1)}, bf16[256,256]{1,0:T(8,128)(2,1)S(1)}, u32[]{:S(2)}, u32[]{:S(2)}) collective-permute-start(bf16[256,256]{1,0:T(8,128)(2,1)S(1)} %get-tuple-element.64), channel_id=1, source_target_pairs={{0,16},{4,20},{8,24},{12,28},{16,0},{20,4},{24,8},{28,12},{1,17},{... | collective-permute-start | bytes 393224 | tf_op jit(solution)/shard_map/ppermute | solution.py:356
  64.6 7.8 %collective-permute-start.17 = (bf16[256,256]{1,0:T(8,128)(2,1)S(1)}, bf16[256,256]{1,0:T(8,128)(2,1)S(1)}, u32[]{:S(2)}, u32[]{:S(2)}) collective-permute-start(bf16[256,256]{1,0:T(8,128)(2,1)S(1)} %get-tuple-element.65), channel_id=1, source_target_pairs={{0,8},{4,12},{8,0},{12,4},{16,24},{20,28},{24,16},{28,20},{1,9},{5... | collective-permute-start | bytes 393224 | tf_op jit(solution)/shard_map/ppermute | solution.py:356
where the time goes:
time: 73.6 us; the launch traced here: 73.4 us
  starting transfers between devices  31.5 us (43%)
  waiting for transfers between devices  29.1 us (40%)
  Pallas kernels  10.2 us (14%)
  local copies, waits for them, and re-layouts  1.05 us (1%)
  other arithmetic  0.88 us (1%)
    ppermute x18, starting transfers between devices, exchanged(): lax.ppermute(block, axis, [(i, i ^ by) for i in range(lax.axis_size(axis))])  31.5 us
    ppermute x18, waiting for transfers between devices, exchanged(): lax.ppermute(block, axis, [(i, i ^ by) for i in range(lax.axis_size(axis))])  29.1 us
    pallas_call x1, Pallas kernels, attend(): pl.pallas_call(functools.partial(attention_kernel, back=back, whole=whole...  8.3 us
  transfers between devices with their start and end apart: 18, of which 13 were waited for; matrix products, arithmetic and copies ran while one was open for 0% of the time, Pallas kernels for 1%

commit v1 on v0

--- a/solution.py
+++ b/solution.py
@@ -53,7 +53,7 @@
         dq_ref,
         *refs,
     ) = refs
-    d_refs, refs = refs[:4], refs[4:]
+    d_refs, refs = refs[: 2 * back + 2], refs[2 * back + 2 :]
     (
         do_ref,
         o_ref,
@@ -194,13 +194,11 @@
     dq_ref[...] = q32[...].astype(jnp.bfloat16)
     for k in range(back + 1):
         mine, other = 2 * pair_of(k) + parity, 2 * pair_of(k) + 1 - parity
-        which, to = (0, back - k) if k > 1 else (2, k)
-        d_refs[which][to, 0:width, :] = d_blocks[mine, 0:width, :] * scale
-        d_refs[which][to, width:, :] = d_blocks[mine, width:, :]
-        d_refs[which + 1][to, 0:width, :] = (d_blocks[other, 0:width, :] * scale).astype(
-            jnp.bfloat16
-        )
-        d_refs[which + 1][to, width:, :] = d_blocks[other, width:, :].astype(jnp.bfloat16)
+        mine_ref, other_ref = d_refs[2 * k], d_refs[2 * k + 1]
+        mine_ref[0:width, :] = d_blocks[mine, 0:width, :] * scale
+        mine_ref[width:, :] = d_blocks[mine, width:, :]
+        other_ref[0:width, :] = (d_blocks[other, 0:width, :] * scale).astype(jnp.bfloat16)
+        other_ref[width:, :] = d_blocks[other, width:, :].astype(jnp.bfloat16)
 
 
 def attend(doc_lengths, queries, own, near, arrived, far, grad_parts, whole):
@@ -228,12 +226,12 @@
             jax.ShapeDtypeStruct((tok, heads, width), jnp.bfloat16),
         ]
         + [
-            jax.ShapeDtypeStruct((size, 2 * width, tok), dtype)
-            for size in (back - 1, 2)
+            jax.ShapeDtypeStruct((2 * width, tok), dtype)
+            for _ in range(back + 1)
             for dtype in (jnp.float32, jnp.bfloat16)
         ],
         in_specs=[smem] + [vmem] * (3 + 2 * back + ranks),
-        out_specs=[vmem] * (ranks + 5),
+        out_specs=[vmem] * (ranks + 2 * back + 3),
         scratch_shapes=[
             pltpu.VMEM((tok, heads * width), jnp.bfloat16),
             pltpu.VMEM((tok, heads * width), jnp.bfloat16),
@@ -303,21 +301,23 @@
     )(*parts)
 
 
-def merge_kernel(mine_ref, other_ref, *block_refs):
-    for k, ref in enumerate(block_refs):
-        ref[...] = (mine_ref[k] + other_ref[k].astype(jnp.float32)).astype(ref.dtype)
-
-
-def merge(mine, other, dtypes):
+def merge_kernel(*refs):
+    total = refs[0][...]
+    for ref in refs[1:-1]:
+        total = total + ref[...].astype(jnp.float32)
+    refs[-1][...] = total.astype(jnp.bfloat16)
+
+
+def merge(*blocks):
     vmem = pl.BlockSpec(memory_space=pltpu.VMEM)
     return pl.pallas_call(
         merge_kernel,
-        out_shape=[jax.ShapeDtypeStruct(mine.shape[1:], dtype) for dtype in dtypes],
-        in_specs=[vmem, vmem],
-        out_specs=[vmem] * len(dtypes),
+        out_shape=jax.ShapeDtypeStruct(blocks[0].shape, jnp.bfloat16),
+        in_specs=[vmem] * len(blocks),
+        out_specs=vmem,
         compiler_params=pltpu.CompilerParams(vmem_limit_bytes=SMALL_VMEM),
         name="merge",
-    )(mine, other)
+    )(*blocks)
 
 
 def finish_kernel(own_ref, *refs):
@@ -366,24 +366,26 @@
     ranks = lax.axis_size("head")
     reach = min((DOC_MOST + tok - 2) // tok, count - 1)
     back = min((reach + 1) // 2, count // 2 - 1)
-    whole = count == 8 and back == 3
+    whole = count == 8 and back == 3 and ranks == 4
     own = jnp.concatenate(
         [key_states.reshape(tok, width), value_states.reshape(tok, width)], axis=0
     )
+    near = exchanged(own, "ctx", 1)
     if whole:
-        across, beside = exchanged(own, "ctx", 4), exchanged(own, "ctx", 2)
+        beside = exchanged(own, "ctx", 2)
+        across = exchanged(own, "ctx", 4)
     else:
         arrived = [shifted(own, 2 * k, count) for k in range(1, back + 1)]
-    near = exchanged(own, "ctx", 1)
     grads = split(grad_attended, ranks)
     grads = [part if k == 0 else exchanged(part, "head", k) for k, part in enumerate(grads)]
     if whole:
         beside, near = after(beside, near)
         far_beside = exchanged(beside, "ctx", 1)
-        across, far_beside, *grads[1:3] = after(across, far_beside, *grads[1:3])
+        across, grads[1] = after(across, grads[1])
         passed = exchanged(across, "ctx", 2)
+        across, far_beside, grads[2] = after(across, far_beside, grads[2])
         far_across = exchanged(across, "ctx", 1)
-        passed, *grads[3:] = after(passed, *grads[3:])
+        passed, grads[3] = after(passed, grads[3])
         far_passed = exchanged(passed, "ctx", 1)
         arrived = [beside, across, passed]
         far = [far_beside, far_across, far_passed]
@@ -393,21 +395,26 @@
         doc_lengths, queries, own, near, arrived, far, grads, whole
     )
 
-    def home(block, k):
-        return exchanged(block, "ctx", 2 * k) if whole else shifted(block, -2 * k, count)
-
-    outs, grad_queries = list(outputs[:ranks]), outputs[ranks]
-    mine_far, other_far, mine_rest, other_rest = outputs[ranks + 1 :]
-    other_far = exchanged(other_far, "ctx", 1)
-    other_rest = exchanged(other_rest, "ctx", 1)
-    outs[1:] = [exchanged(part, "head", k + 1) for k, part in enumerate(outs[1:])]
-    other_far, *outs[1:3] = after(other_far, *outs[1:3])
-    blocks = merge(mine_far, other_far, [jnp.bfloat16] * (back - 1))
-    returned = [home(block, back - n) for n, block in enumerate(blocks)]
-    other_rest, returned[0] = after(other_rest, returned[0])
-    own_block, block = merge(mine_rest, other_rest, [jnp.float32, jnp.bfloat16])
-    returned.append(home(block, 1))
-    grad_keys, grad_values = finish(own_block, returned)
+    outs, grad_queries, parts = list(outputs[:ranks]), outputs[ranks], outputs[ranks + 1 :]
+    mine, other = list(parts[0::2]), list(parts[1::2])
+    outs = [part if k == 0 else exchanged(part, "head", k) for k, part in enumerate(outs)]
+    for k in range(back, -1, -1):
+        if k < back:
+            other[k], other[k + 1] = after(other[k], other[k + 1])
+        other[k] = exchanged(other[k], "ctx", 1)
+    if whole:
+        other[3], outs[1] = after(other[3], outs[1])
+        passed = exchanged(merge(mine[3], other[3]), "ctx", 2)
+        passed, outs[2] = after(passed, outs[2])
+        across = exchanged(merge(mine[2], other[2], passed), "ctx", 4)
+        other[1], outs[3] = after(other[1], outs[3])
+        beside = exchanged(merge(mine[1], other[1]), "ctx", 2)
+        returned = [beside, across]
+    else:
+        returned = [
+            shifted(merge(mine[k], other[k]), -2 * k, count) for k in range(back, 0, -1)
+        ]
+    grad_keys, grad_values = finish(mine[0], [other[0]] + returned)
     attended = join(outs)
     grad_keys = grad_keys.reshape(tok, 1, width)
     grad_values = grad_values.reshape(tok, 1, width)

time: 73.6 us -> 71.4 us (0.970)
  the two profiles are of different devices: /device:TPU:0 before, /device:TPU:25 now
where the time goes in v1:
time: 71.4 us; the launch traced here: 71.2 us
  starting transfers between devices  26.6 us (37%)
  Pallas kernels  23.2 us (32%)
  waiting for transfers between devices  18.8 us (26%)
  local copies, waits for them, and re-layouts  1.05 us (1%)
  other arithmetic  0.88 us (1%)
    ppermute x20, starting transfers between devices, exchanged(): lax.ppermute(block, axis, [(i, i ^ by) for i in range(lax.axis_size(axis))])  26.6 us
    pallas_call x1, Pallas kernels, attend(): pl.pallas_call(functools.partial(attention_kernel, back=back, whole=whole...  21.3 us
    ppermute x20, waiting for transfers between devices, exchanged(): lax.ppermute(block, axis, [(i, i ^ by) for i in range(lax.axis_size(axis))])  18.8 us
  transfers between devices with their start and end apart: 20, of which 8 were waited for; matrix products, arithmetic and copies ran while one was open for 0% of the time, Pallas kernels for 1%

profile of v1, /device:TPU:25, one launch (start us, length us, event | category | flops | bytes accessed | tf_op | source)
XLA Modules:
  0.0 71.2 jit_solution(11770146962431748011)
XLA Ops:
  0.6 0.9 %pad_maximum_fusion.own_ref = bf16[512,128]{1,0:T(8,128)(2,1)S(1)} fusion(bf16[256,128]{1,0:T(8,128)(2,1)} %bitcast.4, bf16[256,128]{1,0:T(8,128)(2,1)} %bitcast.5), kind=kLoop, calls=%fused_computation | loop fusion | flops 262144 | bytes 262144 | tf_op jit(solution)/shard_map/concatenate | solution.py:370
  1.5 1.3 %collective-permute-start.1 = (bf16[512,128]{1,0:T(8,128)(2,1)S(1)}, bf16[512,128]{1,0:T(8,128)(2,1)S(1)}, u32[]{:S(2)}, u32[]{:S(2)}) collective-permute-start(bf16[512,128]{1,0:T(8,128)(2,1)S(1)} %pad_maximum_fusion.own_ref), channel_id=1, source_target_pairs={{0,4},{4,0},{8,12},{12,8},{16,20},{20,16},{24,28},{28,24},{1,5},{5... | collective-permute-start | bytes 393224 | tf_op jit(solution)/shard_map/ppermute | solution.py:356
  2.8 0.2 collective-permute-start
  3.0 0.1 collective-permute-start.2
  3.0 0.0 copy-start
  3.0 1.0 %copy-done = bf16[64,4096]{1,0:T(8,128)(2,1)S(1)} copy-done((bf16[64,4096]{1,0:T(8,128)(2,1)S(1)}, bf16[64,4096]{1,0:T(8,128)(2,1)}, u32[]{:S(2)}) %copy-start) | copy-done | bytes 524312
  4.1 0.0 copy-start.1
  4.1 1.6 %collective-permute-start.3 = (bf16[64,1024]{1,0:T(8,128)(2,1)S(1)}, bf16[64,1024]{1,0:T(8,128)(2,1)S(1)}, u32[]{:S(2)}, u32[]{:S(2)}) collective-permute-start(bf16[64,1024]{1,0:T(8,128)(2,1)S(1)} %get-tuple-element.46), channel_id=1, source_target_pairs={{0,1},{1,0},{2,3},{3,2},{4,5},{5,4},{6,7},{7,6},{8,9},{9,8},{10,11... | collective-permute-start | bytes 393224 | tf_op jit(solution)/shard_map/ppermute | solution.py:356
  5.7 1.2 %collective-permute-start.5 = (bf16[64,1024]{1,0:T(8,128)(2,1)S(1)}, bf16[64,1024]{1,0:T(8,128)(2,1)S(1)}, u32[]{:S(2)}, u32[]{:S(2)}) collective-permute-start(bf16[64,1024]{1,0:T(8,128)(2,1)S(1)} %get-tuple-element.48), channel_id=1, source_target_pairs={{0,2},{1,3},{2,0},{3,1},{4,6},{5,7},{6,4},{7,5},{8,10},{9,11},{10,... | collective-permute-start | bytes 393224 | tf_op jit(solution)/shard_map/ppermute | solution.py:356
  6.9 0.0 collective-permute-done.1.near_ref
  6.9 0.0 copy-start.2
  6.9 1.7 %collective-permute-start.7 = (bf16[64,1024]{1,0:T(8,128)(2,1)S(1)}, bf16[64,1024]{1,0:T(8,128)(2,1)S(1)}, u32[]{:S(2)}, u32[]{:S(2)}) collective-permute-start(bf16[64,1024]{1,0:T(8,128)(2,1)S(1)} %get-tuple-element.50), channel_id=1, source_target_pairs={{0,3},{1,2},{2,1},{3,0},{4,7},{5,6},{6,5},{7,4},{8,11},{9,10},{10,... | collective-permute-start | bytes 393224 | tf_op jit(solution)/shard_map/ppermute | solution.py:356
  8.6 0.0 collective-permute-done.refs_0_
  8.6 1.2 %collective-permute-start.4 = (bf16[512,128]{1,0:T(8,128)(2,1)S(1)}, bf16[512,128]{1,0:T(8,128)(2,1)S(1)}, u32[]{:S(2)}, u32[]{:S(2)}) collective-permute-start(bf16[512,128]{1,0:T(8,128)(2,1)S(1)} %collective-permute-done.refs_0_), channel_id=1, source_target_pairs={{0,4},{4,0},{8,12},{12,8},{16,20},{20,16},{24,28},{28,24},{1,5},{5... | collective-permute-start | bytes 393224 | tf_op jit(solution)/shard_map/ppermute | solution.py:356
  9.8 0.0 collective-permute-done.2.refs_1_
  9.8 0.0 collective-permute-done.3.refs_7_
  9.8 0.2 collective-permute-start.6
  10.0 0.8 %collective-permute-done.5.refs_8_ = bf16[64,1024]{1,0:T(8,128)(2,1)S(1)} collective-permute-done((bf16[64,1024]{1,0:T(8,128)(2,1)S(1)}, bf16[64,1024]{1,0:T(8,128)(2,1)S(1)}, u32[]{:S(2)}, u32[]{:S(2)}) %collective-permute-start.5) | collective-permute-done | bytes 131104 | tf_op jit(solution)/shard_map/ppermute | solution.py:356
  10.8 1.9 %collective-permute-done.4.refs_3_ = bf16[512,128]{1,0:T(8,128)(2,1)S(1)} collective-permute-done((bf16[512,128]{1,0:T(8,128)(2,1)S(1)}, bf16[512,128]{1,0:T(8,128)(2,1)S(1)}, u32[]{:S(2)}, u32[]{:S(2)}) %collective-permute-start.4) | collective-permute-done | bytes 131104 | tf_op jit(solution)/shard_map/ppermute | solution.py:356
  12.7 1.6 %collective-permute-start.8 = (bf16[512,128]{1,0:T(8,128)(2,1)S(1)}, bf16[512,128]{1,0:T(8,128)(2,1)S(1)}, u32[]{:S(2)}, u32[]{:S(2)}) collective-permute-start(bf16[512,128]{1,0:T(8,128)(2,1)S(1)} %collective-permute-done.2.refs_1_), channel_id=1, source_target_pairs={{0,4},{4,0},{8,12},{12,8},{16,20},{20,16},{24,28},{28,24},{1,5},{5... | collective-permute-start | bytes 393224 | tf_op jit(solution)/shard_map/ppermute | solution.py:356
  14.3 0.0 collective-permute-done.7.refs_9_
  14.3 0.0 collective-permute-done.6.refs_2_
  14.3 0.1 collective-permute-start.9
  14.4 2.6 %collective-permute-done.8.refs_4_ = bf16[512,128]{1,0:T(8,128)(2,1)S(1)} collective-permute-done((bf16[512,128]{1,0:T(8,128)(2,1)S(1)}, bf16[512,128]{1,0:T(8,128)(2,1)S(1)}, u32[]{:S(2)}, u32[]{:S(2)}) %collective-permute-start.8) | collective-permute-done | bytes 131104 | tf_op jit(solution)/shard_map/ppermute | solution.py:356
  16.9 1.5 %collective-permute-done.9.refs_5_ = bf16[512,128]{1,0:T(8,128)(2,1)S(1)} collective-permute-done((bf16[512,128]{1,0:T(8,128)(2,1)S(1)}, bf16[512,128]{1,0:T(8,128)(2,1)S(1)}, u32[]{:S(2)}, u32[]{:S(2)}) %collective-permute-start.9) | collective-permute-done | bytes 131104 | tf_op jit(solution)/shard_map/ppermute | solution.py:356
  18.4 0.0 copy-done.1
  18.4 0.0 copy-done.2
  18.4 21.3 %attention.1 = (bf16[64,1024]{1,0:T(8,128)(2,1)S(1)}, bf16[64,1024]{1,0:T(8,128)(2,1)S(1)}, bf16[64,1024]{1,0:T(8,128)(2,1)S(1)}, bf16[64,1024]{1,0:T(8,128)(2,1...) custom-call(s32[8]{0:T(128)S(1)} %copy-done.2, ...), custom_call_target="tpu_custom_call" | custom-call | flops 7516192768 | bytes 4194304 | tf_op jit(solution)/shard_map/attention/pallas_call | solution.py:214
  39.7 4.8 %collective-permute-start.10 = (bf16[256,256]{1,0:T(8,128)(2,1)S(1)}, bf16[256,256]{1,0:T(8,128)(2,1)S(1)}, u32[]{:S(2)}, u32[]{:S(2)}) collective-permute-start(bf16[256,256]{1,0:T(8,128)(2,1)S(1)} %get-tuple-element.59), channel_id=1, source_target_pairs={{0,4},{4,0},{8,12},{12,8},{16,20},{20,16},{24,28},{28,24},{1,5},{5... | collective-permute-start | bytes 393224 | tf_op jit(solution)/shard_map/ppermute | solution.py:356
  44.5 2.7 %collective-permute-start.11 = (bf16[64,1024]{1,0:T(8,128)(2,1)S(1)}, bf16[64,1024]{1,0:T(8,128)(2,1)S(1)}, u32[]{:S(2)}, u32[]{:S(2)}) collective-permute-start(bf16[64,1024]{1,0:T(8,128)(2,1)S(1)} %get-tuple-element.61), channel_id=1, source_target_pairs={{0,1},{1,0},{2,3},{3,2},{4,5},{5,4},{6,7},{7,6},{8,9},{9,8},{10,11... | collective-permute-start | bytes 393224 | tf_op jit(solution)/shard_map/ppermute | solution.py:356
  47.2 0.0 collective-permute-done.10.refs_1_
  47.2 1.1 %collective-permute-start.14 = (bf16[256,256]{1,0:T(8,128)(2,1)S(1)}, bf16[256,256]{1,0:T(8,128)(2,1)S(1)}, u32[]{:S(2)}, u32[]{:S(2)}) collective-permute-start(bf16[256,256]{1,0:T(8,128)(2,1)S(1)} %get-tuple-element.69), channel_id=1, source_target_pairs={{0,4},{4,0},{8,12},{12,8},{16,20},{20,16},{24,28},{28,24},{1,5},{5... | collective-permute-start | bytes 393224 | tf_op jit(solution)/shard_map/ppermute | solution.py:356
  48.3 0.0 collective-permute-start.13
  48.3 0.0 collective-permute-done.11.refs_1_
  48.3 0.1 collective-permute-start.12
  48.4 2.6 %collective-permute-done.14.refs_1_ = bf16[256,256]{1,0:T(8,128)(2,1)S(1)} collective-permute-done((bf16[256,256]{1,0:T(8,128)(2,1)S(1)}, bf16[256,256]{1,0:T(8,128)(2,1)S(1)}, u32[]{:S(2)}, u32[]{:S(2)}) %collective-permute-start.14) | collective-permute-done | bytes 131104 | tf_op jit(solution)/shard_map/ppermute | solution.py:356
  51.0 1.6 %collective-permute-start.15 = (bf16[256,256]{1,0:T(8,128)(2,1)S(1)}, bf16[256,256]{1,0:T(8,128)(2,1)S(1)}, u32[]{:S(2)}, u32[]{:S(2)}) collective-permute-start(bf16[256,256]{1,0:T(8,128)(2,1)S(1)} %get-tuple-element.70), channel_id=1, source_target_pairs={{0,4},{4,0},{8,12},{12,8},{16,20},{20,16},{24,28},{28,24},{1,5},{5... | collective-permute-start | bytes 393224 | tf_op jit(solution)/shard_map/ppermute | solution.py:356
  52.6 7.1 %collective-permute-start.16 = (bf16[64,1024]{1,0:T(8,128)(2,1)S(1)}, bf16[64,1024]{1,0:T(8,128)(2,1)S(1)}, u32[]{:S(2)}, u32[]{:S(2)}) collective-permute-start(bf16[64,1024]{1,0:T(8,128)(2,1)S(1)} %get-tuple-element.72), channel_id=1, source_target_pairs={{0,3},{1,2},{2,1},{3,0},{4,7},{5,6},{6,5},{7,4},{8,11},{9,10},{10,... | collective-permute-start | bytes 393224 | tf_op jit(solution)/shard_map/ppermute | solution.py:356
  59.6 0.0 collective-permute-done.13.refs_2_
  59.6 0.0 collective-permute-done.12.refs_2_
  59.7 0.1 collective-permute-start.19
  59.8 0.0 collective-permute-done.15.refs_1_
  59.8 0.1 collective-permute-start.17
  59.9 3.9 %collective-permute-done.16.refs_3_ = bf16[64,1024]{1,0:T(8,128)(2,1)S(1)} collective-permute-done((bf16[64,1024]{1,0:T(8,128)(2,1)S(1)}, bf16[64,1024]{1,0:T(8,128)(2,1)S(1)}, u32[]{:S(2)}, u32[]{:S(2)}) %collective-permute-start.16) | collective-permute-done | bytes 131104 | tf_op jit(solution)/shard_map/ppermute | solution.py:356
  63.8 0.1 collective-permute-start.18
  63.9 0.8 %join.1 = bf16[64,4096]{1,0:T(8,128)(2,1)} custom-call(bf16[64,1024]{1,0:T(8,128)(2,1)S(1)} %get-tuple-element.57.refs_0_, bf16[64,1024]{1,0:T(8,128)(2,1)S(1)} %collective-permute-done.11.refs_1_, bf16[64,1024]{1,0:T(8,128)(2,1)S(1)} %collective-permute-done.13.refs_2_, bf16[64,1024]{1,0:T(8,128)(2,1)S(1)} %collective-permute-done.16.refs_3_), custom_call_target="tpu_custom_call" | custom-call | tf_op jit(solution)/shard_map/join/pallas_call | solution.py:294
  64.8 2.8 %collective-permute-done.19.refs_2_ = bf16[256,256]{1,0:T(8,128)(2,1)S(1)} collective-permute-done((bf16[256,256]{1,0:T(8,128)(2,1)S(1)}, bf16[256,256]{1,0:T(8,128)(2,1)S(1)}, u32[]{:S(2)}, u32[]{:S(2)}) %collective-permute-start.19) | collective-permute-done | bytes 131104 | tf_op jit(solution)/shard_map/ppermute | solution.py:356
  67.5 0.0 collective-permute-done.17.refs_0_
  67.5 2.8 %collective-permute-done.18.refs_1_ = bf16[256,256]{1,0:T(8,128)(2,1)S(1)} collective-permute-done((bf16[256,256]{1,0:T(8,128)(2,1)S(1)}, bf16[256,256]{1,0:T(8,128)(2,1)S(1)}, u32[]{:S(2)}, u32[]{:S(2)}) %collective-permute-start.18) | collective-permute-done | bytes 131104 | tf_op jit(solution)/shard_map/ppermute | solution.py:356
  70.3 0.9 %finish.1 = (bf16[256,128]{1,0:T(8,128)(2,1)}, bf16[256,128]{1,0:T(8,128)(2,1)}) custom-call(f32[256,256]{1,0:T(8,128)S(1)} %get-tuple-element.75.own_ref, bf16[256,256]{1,0:T(8,128)(2,1)S(1)} %collective-permute-done.17.refs_0_, bf16[256,256]{1,0:T(8,128)(2,1)S(1)} %collective-permute-done.18.refs_1_, bf16[256,256]{1,0:T(8,128)(2,1)S(1)} %collective-permute-done.19.refs_2_), custom_call_target="tpu_custom_call" | custom-call | tf_op jit(solution)/shard_map/finish/pallas_call | solution.py:340
  (4 shorter events, 0.1 us)
Async XLA Ops:
  1.5 5.4 %collective-permute-start.1 = (bf16[512,128]{1,0:T(8,128)(2,1)S(1)}, bf16[512,128]{1,0:T(8,128)(2,1)S(1)}, u32[]{:S(2)}, u32[]{:S(2)}) collective-permute-start(bf16[512,128]{1,0:T(8,128)(2,1)S(1)} %pad_maximum_fusion.own_ref), channel_id=1, source_target_pairs={{0,4},{4,0},{8,12},{12,8},{16,20},{20,16},{24,28},{28,24},{1,5},{5... | collective-permute-start | bytes 393224 | tf_op jit(solution)/shard_map/ppermute | solution.py:356
  2.8 5.8 %collective-permute-start = (bf16[512,128]{1,0:T(8,128)(2,1)S(1)}, bf16[512,128]{1,0:T(8,128)(2,1)S(1)}, u32[]{:S(2)}, u32[]{:S(2)}) collective-permute-start(bf16[512,128]{1,0:T(8,128)(2,1)S(1)} %pad_maximum_fusion.own_ref), channel_id=1, source_target_pairs={{0,8},{4,12},{8,0},{12,4},{16,24},{20,28},{24,16},{28,20},{1,9},{5... | collective-permute-start | bytes 393224 | tf_op jit(solution)/shard_map/ppermute | solution.py:356
  3.0 6.8 %collective-permute-start.2 = (bf16[512,128]{1,0:T(8,128)(2,1)S(1)}, bf16[512,128]{1,0:T(8,128)(2,1)S(1)}, u32[]{:S(2)}, u32[]{:S(2)}) collective-permute-start(bf16[512,128]{1,0:T(8,128)(2,1)S(1)} %pad_maximum_fusion.own_ref), channel_id=1, source_target_pairs={{0,16},{4,20},{8,24},{12,28},{16,0},{20,4},{24,8},{28,12},{1,17},{... | collective-permute-start | bytes 393224 | tf_op jit(solution)/shard_map/ppermute | solution.py:356
  3.0 1.0 %copy-start = (bf16[64,4096]{1,0:T(8,128)(2,1)S(1)}, bf16[64,4096]{1,0:T(8,128)(2,1)}, u32[]{:S(2)}) copy-start(bf16[64,4096]{1,0:T(8,128)(2,1)} %grad_ref.1) | copy-start | bytes 1572868
  4.1 14.3 %copy-start.1 = (bf16[256,8,128]{2,1,0:T(8,128)(2,1)S(1)}, bf16[256,8,128]{2,1,0:T(8,128)(2,1)}, u32[]{:S(2)}) copy-start(bf16[256,8,128]{2,1,0:T(8,128)(2,1)} %q_ref.1) | copy-start | bytes 1572868
  4.1 5.7 %collective-permute-start.3 = (bf16[64,1024]{1,0:T(8,128)(2,1)S(1)}, bf16[64,1024]{1,0:T(8,128)(2,1)S(1)}, u32[]{:S(2)}, u32[]{:S(2)}) collective-permute-start(bf16[64,1024]{1,0:T(8,128)(2,1)S(1)} %get-tuple-element.46), channel_id=1, source_target_pairs={{0,1},{1,0},{2,3},{3,2},{4,5},{5,4},{6,7},{7,6},{8,9},{9,8},{10,11... | collective-permute-start | bytes 393224 | tf_op jit(solution)/shard_map/ppermute | solution.py:356
  5.7 5.1 %collective-permute-start.5 = (bf16[64,1024]{1,0:T(8,128)(2,1)S(1)}, bf16[64,1024]{1,0:T(8,128)(2,1)S(1)}, u32[]{:S(2)}, u32[]{:S(2)}) collective-permute-start(bf16[64,1024]{1,0:T(8,128)(2,1)S(1)} %get-tuple-element.48), channel_id=1, source_target_pairs={{0,2},{1,3},{2,0},{3,1},{4,6},{5,7},{6,4},{7,5},{8,10},{9,11},{10,... | collective-permute-start | bytes 393224 | tf_op jit(solution)/shard_map/ppermute | solution.py:356
  6.9 11.5 %copy-start.2 = (s32[8]{0:T(128)S(1)}, s32[8]{0:T(128)}, u32[]{:S(2)}) copy-start(s32[8]{0:T(128)} %doc_ref.1) | copy-start | bytes 100
  6.9 7.3 %collective-permute-start.7 = (bf16[64,1024]{1,0:T(8,128)(2,1)S(1)}, bf16[64,1024]{1,0:T(8,128)(2,1)S(1)}, u32[]{:S(2)}, u32[]{:S(2)}) collective-permute-start(bf16[64,1024]{1,0:T(8,128)(2,1)S(1)} %get-tuple-element.50), channel_id=1, source_target_pairs={{0,3},{1,2},{2,1},{3,0},{4,7},{5,6},{6,5},{7,4},{8,11},{9,10},{10,... | collective-permute-start | bytes 393224 | tf_op jit(solution)/shard_map/ppermute | solution.py:356
  8.6 4.1 %collective-permute-start.4 = (bf16[512,128]{1,0:T(8,128)(2,1)S(1)}, bf16[512,128]{1,0:T(8,128)(2,1)S(1)}, u32[]{:S(2)}, u32[]{:S(2)}) collective-permute-start(bf16[512,128]{1,0:T(8,128)(2,1)S(1)} %collective-permute-done.refs_0_), channel_id=1, source_target_pairs={{0,4},{4,0},{8,12},{12,8},{16,20},{20,16},{24,28},{28,24},{1,5},{5... | collective-permute-start | bytes 393224 | tf_op jit(solution)/shard_map/ppermute | solution.py:356
  9.8 4.4 %collective-permute-start.6 = (bf16[512,128]{1,0:T(8,128)(2,1)S(1)}, bf16[512,128]{1,0:T(8,128)(2,1)S(1)}, u32[]{:S(2)}, u32[]{:S(2)}) collective-permute-start(bf16[512,128]{1,0:T(8,128)(2,1)S(1)} %collective-permute-done.2.refs_1_), channel_id=1, source_target_pairs={{0,8},{4,12},{8,0},{12,4},{16,24},{20,28},{24,16},{28,20},{1,9},{5... | collective-permute-start | bytes 393224 | tf_op jit(solution)/shard_map/ppermute | solution.py:356
  12.7 4.2 %collective-permute-start.8 = (bf16[512,128]{1,0:T(8,128)(2,1)S(1)}, bf16[512,128]{1,0:T(8,128)(2,1)S(1)}, u32[]{:S(2)}, u32[]{:S(2)}) collective-permute-start(bf16[512,128]{1,0:T(8,128)(2,1)S(1)} %collective-permute-done.2.refs_1_), channel_id=1, source_target_pairs={{0,4},{4,0},{8,12},{12,8},{16,20},{20,16},{24,28},{28,24},{1,5},{5... | collective-permute-start | bytes 393224 | tf_op jit(solution)/shard_map/ppermute | solution.py:356
  14.3 4.1 %collective-permute-start.9 = (bf16[512,128]{1,0:T(8,128)(2,1)S(1)}, bf16[512,128]{1,0:T(8,128)(2,1)S(1)}, u32[]{:S(2)}, u32[]{:S(2)}) collective-permute-start(bf16[512,128]{1,0:T(8,128)(2,1)S(1)} %collective-permute-done.6.refs_2_), channel_id=1, source_target_pairs={{0,4},{4,0},{8,12},{12,8},{16,20},{20,16},{24,28},{28,24},{1,5},{5... | collective-permute-start | bytes 393224 | tf_op jit(solution)/shard_map/ppermute | solution.py:356
  39.7 7.5 %collective-permute-start.10 = (bf16[256,256]{1,0:T(8,128)(2,1)S(1)}, bf16[256,256]{1,0:T(8,128)(2,1)S(1)}, u32[]{:S(2)}, u32[]{:S(2)}) collective-permute-start(bf16[256,256]{1,0:T(8,128)(2,1)S(1)} %get-tuple-element.59), channel_id=1, source_target_pairs={{0,4},{4,0},{8,12},{12,8},{16,20},{20,16},{24,28},{28,24},{1,5},{5... | collective-permute-start | bytes 393224 | tf_op jit(solution)/shard_map/ppermute | solution.py:356
  44.5 3.8 %collective-permute-start.11 = (bf16[64,1024]{1,0:T(8,128)(2,1)S(1)}, bf16[64,1024]{1,0:T(8,128)(2,1)S(1)}, u32[]{:S(2)}, u32[]{:S(2)}) collective-permute-start(bf16[64,1024]{1,0:T(8,128)(2,1)S(1)} %get-tuple-element.61), channel_id=1, source_target_pairs={{0,1},{1,0},{2,3},{3,2},{4,5},{5,4},{6,7},{7,6},{8,9},{9,8},{10,11... | collective-permute-start | bytes 393224 | tf_op jit(solution)/shard_map/ppermute | solution.py:356
  47.2 3.8 %collective-permute-start.14 = (bf16[256,256]{1,0:T(8,128)(2,1)S(1)}, bf16[256,256]{1,0:T(8,128)(2,1)S(1)}, u32[]{:S(2)}, u32[]{:S(2)}) collective-permute-start(bf16[256,256]{1,0:T(8,128)(2,1)S(1)} %get-tuple-element.69), channel_id=1, source_target_pairs={{0,4},{4,0},{8,12},{12,8},{16,20},{20,16},{24,28},{28,24},{1,5},{5... | collective-permute-start | bytes 393224 | tf_op jit(solution)/shard_map/ppermute | solution.py:356
  48.3 11.3 %collective-permute-start.13 = (bf16[64,1024]{1,0:T(8,128)(2,1)S(1)}, bf16[64,1024]{1,0:T(8,128)(2,1)S(1)}, u32[]{:S(2)}, u32[]{:S(2)}) collective-permute-start(bf16[64,1024]{1,0:T(8,128)(2,1)S(1)} %get-tuple-element.65), channel_id=1, source_target_pairs={{0,2},{1,3},{2,0},{3,1},{4,6},{5,7},{6,4},{7,5},{8,10},{9,11},{10,... | collective-permute-start | bytes 393224 | tf_op jit(solution)/shard_map/ppermute | solution.py:356
  48.3 11.3 %collective-permute-start.12 = (bf16[256,256]{1,0:T(8,128)(2,1)S(1)}, bf16[256,256]{1,0:T(8,128)(2,1)S(1)}, u32[]{:S(2)}, u32[]{:S(2)}) collective-permute-start(bf16[256,256]{1,0:T(8,128)(2,1)S(1)} %merge.3), channel_id=1, source_target_pairs={{0,8},{4,12},{8,0},{12,4},{16,24},{20,28},{24,16},{28,20},{1,9},{5... | collective-permute-start | bytes 393224 | tf_op jit(solution)/shard_map/ppermute | solution.py:356
  51.0 8.8 %collective-permute-start.15 = (bf16[256,256]{1,0:T(8,128)(2,1)S(1)}, bf16[256,256]{1,0:T(8,128)(2,1)S(1)}, u32[]{:S(2)}, u32[]{:S(2)}) collective-permute-start(bf16[256,256]{1,0:T(8,128)(2,1)S(1)} %get-tuple-element.70), channel_id=1, source_target_pairs={{0,4},{4,0},{8,12},{12,8},{16,20},{20,16},{24,28},{28,24},{1,5},{5... | collective-permute-start | bytes 393224 | tf_op jit(solution)/shard_map/ppermute | solution.py:356
  52.6 11.2 %collective-permute-start.16 = (bf16[64,1024]{1,0:T(8,128)(2,1)S(1)}, bf16[64,1024]{1,0:T(8,128)(2,1)S(1)}, u32[]{:S(2)}, u32[]{:S(2)}) collective-permute-start(bf16[64,1024]{1,0:T(8,128)(2,1)S(1)} %get-tuple-element.72), channel_id=1, source_target_pairs={{0,3},{1,2},{2,1},{3,0},{4,7},{5,6},{6,5},{7,4},{8,11},{9,10},{10,... | collective-permute-start | bytes 393224 | tf_op jit(solution)/shard_map/ppermute | solution.py:356
  59.7 7.8 %collective-permute-start.19 = (bf16[256,256]{1,0:T(8,128)(2,1)S(1)}, bf16[256,256]{1,0:T(8,128)(2,1)S(1)}, u32[]{:S(2)}, u32[]{:S(2)}) collective-permute-start(bf16[256,256]{1,0:T(8,128)(2,1)S(1)} %merge.5), channel_id=1, source_target_pairs={{0,16},{4,20},{8,24},{12,28},{16,0},{20,4},{24,8},{28,12},{1,17},{... | collective-permute-start | bytes 393224 | tf_op jit(solution)/shard_map/ppermute | solution.py:356
  59.8 7.8 %collective-permute-start.17 = (bf16[256,256]{1,0:T(8,128)(2,1)S(1)}, bf16[256,256]{1,0:T(8,128)(2,1)S(1)}, u32[]{:S(2)}, u32[]{:S(2)}) collective-permute-start(bf16[256,256]{1,0:T(8,128)(2,1)S(1)} %get-tuple-element.76), channel_id=1, source_target_pairs={{0,4},{4,0},{8,12},{12,8},{16,20},{20,16},{24,28},{28,24},{1,5},{5... | collective-permute-start | bytes 393224 | tf_op jit(solution)/shard_map/ppermute | solution.py:356
  63.8 6.5 %collective-permute-start.18 = (bf16[256,256]{1,0:T(8,128)(2,1)S(1)}, bf16[256,256]{1,0:T(8,128)(2,1)S(1)}, u32[]{:S(2)}, u32[]{:S(2)}) collective-permute-start(bf16[256,256]{1,0:T(8,128)(2,1)S(1)} %merge.4), channel_id=1, source_target_pairs={{0,8},{4,12},{8,0},{12,4},{16,24},{20,28},{24,16},{28,20},{1,9},{5... | collective-permute-start | bytes 393224 | tf_op jit(solution)/shard_map/ppermute | solution.py:356
